TPU v7x, 32 devices: a whole 2x2x4 slice. The times are simulated.
32 devices in a mesh: runs: 2 (over x), gy: 16 (over z, y, core).
Axes of the slice: x: 2, y: 2, z: 4, core: 2. Of those that a mesh axis runs over, the one named last changes fastest.
Arguments:
- depth: float32 [1024, 1920], P(('runs', 'gy')), parts along dimension 0, may hold values from 0.02 to 3
- flux_east: float32 [1024, 1920], P(('runs', 'gy')), parts along dimension 0, may hold values from -2 to 2
- flux_south: float32 [1024, 1920], P(('runs', 'gy')), parts along dimension 0, may hold values from -2 to 2
- river_section: float32 [4096], P(('runs', 'gy')), parts along dimension 0, may hold values from 0 to 2
- bed_level: float32 [512, 1920], P('gy'), may hold values from -3 to 3
- rough_class: int32 [512, 1920], P('gy'), may hold values from 0 to 7
- manning_table: float32 [8], replicated, may hold values from 0.02 to 0.15
- bank_cell: int32 [4, 2048], P(None, 'gy'), may hold values from 0 to 983039, as said below
Outputs:
- depth_out: float32 [1024, 1920], P(('runs', 'gy')), parts along dimension 0
- east_out: float32 [1024, 1920], P(('runs', 'gy')), parts along dimension 0
- south_out: float32 [1024, 1920], P(('runs', 'gy')), parts along dimension 0
- section_out: float32 [4096], P(('runs', 'gy')), parts along dimension 0
There are 2 independent parts, one for each index of `runs`. A program takes and returns all parts, laid end to end along the dimension named above; an argument that names none is the same for every part. Nothing has to cross between parts.
Inputs may be any that keep to these rules, and one draw needn't show every extreme that they name: `bank_cell`: the 4 corridor cells of a node are consecutive flat indices row * 1920 + column within one map row. Node n is owned by gy index o = n // 128, and all its corridor cells lie in map rows from max((o - 1) * 32, 0) to min((o + 2) * 32, 512) - 1.
All inputs are finite; a program needn't handle non-finite values.
Results may differ from a plain program's by a relative error of at most 0.00013.
Values sent between devices are 32-bit elements; how exact they have to be, the bound alone decides.
A program may use at most 64 MiB of HBM per device.

v0:
```python
import jax
import jax.numpy as jnp
from jax import lax
from jax.experimental import pallas as pl
from jax.experimental.pallas import tpu as pltpu
from jax.sharding import PartitionSpec as P

STEPS = 4
HALO = STEPS
LANES = 128

GRAV = 9.81
TSTEP = 8.0
CELL = 90.0
FLOOR = 0.05
BANK_COEF = 200.0
CELL_AREA = 8100.0
NODE_AREA = 20000.0

MESH = pl.DeviceIdType.MESH
VMEM_BYTES = 40 * 1024 * 1024
FAR = -float(1 << 24)


def send(src, dst, send_sem, recv_sem, target):
    return pltpu.make_async_remote_copy(
        src_ref=src,
        dst_ref=dst,
        send_sem=send_sem,
        recv_sem=recv_sem,
        device_id={"gy": target},
        device_id_type=MESH,
    )


def exchange_kernel(*refs):
    firsts, lasts = refs[0:5], refs[5:10]
    section, cells = refs[10:12]
    below_out, above_out, nodes_out = refs[12:15]
    up, down, below, above, mine, nodes, ssem, rsem, nssem, nrsem = refs[15:]
    me = lax.axis_index("gy")
    count = lax.axis_size("gy")
    offsets = (-2, -1, 1, 2)

    def there(offset):
        return (me + offset >= 0) & (me + offset < count)

    barrier = pltpu.get_barrier_semaphore()
    for offset in offsets:
        @pl.when(there(offset))
        def _():
            pl.semaphore_signal(
                barrier, inc=1, device_id={"gy": me + offset}, device_id_type=MESH
            )

    for i in range(5):
        up[i] = firsts[i][:HALO, :].astype(jnp.float32)
        down[i] = lasts[i][8 - HALO :, :].astype(jnp.float32)
    mine[0:1, :] = section[...]
    mine[1:2, :] = cells[0:1, :].astype(jnp.float32)

    pl.semaphore_wait(barrier, jnp.minimum(me, 2) + jnp.minimum(count - 1 - me, 2))

    to_prev = send(up, below, ssem.at[0], rsem.at[0], me - 1)
    to_next = send(down, above, ssem.at[1], rsem.at[1], me + 1)
    to_nodes = [
        send(mine, nodes.at[i], nssem.at[i], nrsem.at[i], me - offset)
        for i, offset in enumerate(offsets)
    ]

    for i, offset in enumerate(offsets):
        @pl.when(there(-offset))
        def _():
            to_nodes[i].start()

    @pl.when(there(-1))
    def _():
        to_prev.start()

    @pl.when(there(1))
    def _():
        to_next.start()

    nodes_out[2] = mine[...]
    for i, offset in enumerate(offsets):
        slot = offset + 2

        @pl.when(there(offset))
        def _():
            to_nodes[i].wait_recv()
            nodes_out[slot] = nodes[i]

        @pl.when(jnp.logical_not(there(offset)))
        def _():
            nodes_out[slot, 0:1, :] = jnp.zeros((1, nodes_out.shape[2]), jnp.float32)
            nodes_out[slot, 1:2, :] = jnp.full((1, nodes_out.shape[2]), FAR, jnp.float32)

    @pl.when(there(1))
    def _():
        to_prev.wait_recv()
        below_out[...] = below[...]

    @pl.when(jnp.logical_not(there(1)))
    def _():
        below_out[...] = jnp.zeros_like(below_out)

    @pl.when(there(-1))
    def _():
        to_next.wait_recv()
        above_out[...] = above[...]

    @pl.when(jnp.logical_not(there(-1)))
    def _():
        above_out[...] = jnp.zeros_like(above_out)

    @pl.when(there(-1))
    def _():
        to_prev.wait_send()

    @pl.when(there(1))
    def _():
        to_next.wait_send()

    for i, offset in enumerate(offsets):
        @pl.when(there(-offset))
        def _():
            to_nodes[i].wait_send()


def exchange(arrays, section, bank_cell):
    rows, columns = arrays[0].shape
    owned = section.shape[1]
    strip = (5, HALO, columns)
    first = pl.BlockSpec((8, columns), lambda i: (0, 0))
    last = pl.BlockSpec((8, columns), lambda i: (rows // 8 - 1, 0))
    whole = lambda *shape: pl.BlockSpec(shape, lambda i: (0,) * len(shape))
    return pl.pallas_call(
        exchange_kernel,
        grid=(1,),
        out_shape=[
            jax.ShapeDtypeStruct(strip, jnp.float32),
            jax.ShapeDtypeStruct(strip, jnp.float32),
            jax.ShapeDtypeStruct((5, 2, owned), jnp.float32),
        ],
        in_specs=[first] * 5
        + [last] * 5
        + [whole(1, owned), whole(*bank_cell.shape)],
        out_specs=[whole(*strip), whole(*strip), whole(5, 2, owned)],
        scratch_shapes=[pltpu.VMEM(strip, jnp.float32)] * 4
        + [
            pltpu.VMEM((2, owned), jnp.float32),
            pltpu.VMEM((4, 2, owned), jnp.float32),
            pltpu.SemaphoreType.DMA((2,)),
            pltpu.SemaphoreType.DMA((2,)),
            pltpu.SemaphoreType.DMA((4,)),
            pltpu.SemaphoreType.DMA((4,)),
        ],
        compiler_params=pltpu.CompilerParams(collective_id=0, has_side_effects=True),
        name="exchange",
    )(*arrays, *arrays, section, bank_cell)


def thirds(value):
    high = value.astype(jnp.bfloat16).astype(jnp.float32)
    rest = value - high
    mid = rest.astype(jnp.bfloat16).astype(jnp.float32)
    return high, mid, rest - mid


def steps_kernel(
    table,
    pos,
    depth,
    flux_east,
    flux_south,
    bed_in,
    rough_in,
    below,
    above,
    nodes,
    depth_out,
    east_out,
    south_out,
    part_out,
    surf,
    fe,
    fs,
    bed,
    mann,
    max_e,
    max_s,
    drag_e,
    drag_s,
    tally,
    number,
    number4,
    gained,
    partial,
):
    me = pos[0]
    tiles = pos[1]
    rows, columns = depth.shape
    ext = rows + 2 * HALO
    chunks = columns // LANES
    owned = nodes.shape[2]
    keep = 1.0 - TSTEP * BANK_COEF * 4.0 / NODE_AREA
    gain = TSTEP * BANK_COEF / NODE_AREA
    into = TSTEP * BANK_COEF / CELL_AREA

    def at(chunk, shift=0):
        start = LANES * (chunk + 1) + shift
        return slice(start, start + LANES)

    def south(value):
        return pltpu.roll(value, ext - 1, 0)

    def north(value):
        return pltpu.roll(value, 1, 0)

    for ref in (surf, fe, bed, mann, tally, number):
        ref[:, :LANES] = jnp.zeros((ext, LANES), jnp.float32)
        ref[:, LANES * (chunks + 1) :] = jnp.zeros((ext, LANES), jnp.float32)

    def extended(source, index, chunk):
        lanes = slice(LANES * chunk, LANES * (chunk + 1))
        return jnp.concatenate(
            [source[:, lanes].astype(jnp.float32), below[index, :, lanes], above[index, :, lanes]],
            axis=0,
        )

    row_id = lax.broadcasted_iota(jnp.int32, (ext, LANES), 0)
    lane_id = lax.broadcasted_iota(jnp.int32, (ext, LANES), 1)
    south_open = jnp.logical_not(
        ((row_id == ext - 1) & (me == 0)) | ((row_id == rows - 1) & (me == tiles - 1))
    )

    for c in range(chunks):
        bed_c = extended(bed_in, 3, c)
        bed[:, at(c)] = bed_c
        surf[:, at(c)] = extended(depth, 0, c) + bed_c
        fe[:, at(c)] = extended(flux_east, 1, c)
        fs[:, at(c)] = extended(flux_south, 2, c)
        rough = extended(rough_in, 4, c)
        value = jnp.zeros((ext, LANES), jnp.float32)
        for klass in range(table.shape[0]):
            value = jnp.where(rough == float(klass), table[klass], value)
        mann[:, at(c)] = value
    for c in range(chunks):
        bed_c, mann_c = bed[:, at(c)], mann[:, at(c)]
        max_e[:, at(c)] = jnp.maximum(bed_c, bed[:, at(c, 1)])
        max_s[:, at(c)] = jnp.maximum(bed_c, south(bed_c))
        mean_e = 0.5 * (mann_c + mann[:, at(c, 1)])
        mean_s = 0.5 * (mann_c + south(mann_c))
        drag_e[:, at(c)] = GRAV * TSTEP * mean_e * mean_e
        drag_s[:, at(c)] = GRAV * TSTEP * mean_s * mean_s
        gained[:, at(c)] = jnp.zeros((ext, LANES), jnp.float32)

    section = jnp.concatenate([nodes[i, 0:1, :] for i in range(5)], axis=1)
    cell = jnp.concatenate([nodes[i, 1:2, :] for i in range(5)], axis=1).astype(jnp.int32)
    local = cell - (me * rows - HALO) * columns
    valid = (local >= 0) & (local < ext * columns)
    local = jnp.where(valid, local, 0)
    from_top = ((local.astype(jnp.float32) + 0.5) * (1.0 / columns)).astype(jnp.int32)
    column = local - from_top * columns
    row = jnp.where(from_top < HALO, from_top + ext - HALO, from_top - HALO)
    place = jnp.where(valid, (column >> 7) * ext + row, -1)
    lane = column & (LANES - 1)
    total = 5 * owned
    blocks = chunks * ext
    blocks_pad = -(-blocks // LANES) * LANES
    hit = (lax.broadcasted_iota(jnp.int32, (blocks_pad, total), 0) == place)
    hit = jnp.where(hit, 1.0, 0.0).astype(jnp.bfloat16)
    lane_hit = lax.broadcasted_iota(jnp.int32, (LANES, total), 0) == lane
    parts = [jnp.where(lane_hit, part, 0.0) for part in thirds(section)]
    parts.append(jnp.where(lane_hit, 1.0, 0.0))
    weights = jnp.concatenate(parts, axis=0).astype(jnp.bfloat16)
    spread = lax.dot_general(
        hit, weights, (((1,), (1,)), ((), ())), preferred_element_type=jnp.float32
    )
    for c in range(chunks):
        block = spread[c * ext : (c + 1) * ext]
        tally[:, at(c)] = (
            block[:, :LANES] + block[:, LANES : 2 * LANES] + block[:, 2 * LANES : 3 * LANES]
        )
        number[:, at(c)] = block[:, 3 * LANES :]
    for c in range(chunks):
        number4[:, at(c)] = (
            number[:, at(c)] + number[:, at(c, -1)] + number[:, at(c, -2)] + number[:, at(c, -3)]
        )

    def face(flux, surf_a, surf_b, bed_top, drag):
        flow_depth = jnp.maximum(jnp.maximum(surf_a, surf_b) - bed_top, FLOOR)
        driven = flux - (GRAV * TSTEP / CELL) * flow_depth * (surf_b - surf_a)
        damping = 1.0 + drag * jnp.abs(flux) * jnp.exp(jnp.log(flow_depth) * (-7.0 / 3.0))
        return driven / damping

    def substep(_, carry):
        for c in reversed(range(chunks)):
            here = surf[:, at(c)]
            east = surf[:, at(c, 1)]
            new_east = face(fe[:, at(c)], here, east, max_e[:, at(c)], drag_e[:, at(c)])
            if c == chunks - 1:
                new_east = jnp.where(lane_id == LANES - 1, 0.0, new_east)
            fe[:, at(c)] = new_east
            new_south = face(
                fs[:, at(c)], here, south(here), max_s[:, at(c)], drag_s[:, at(c)]
            )
            new_south = jnp.where(south_open, new_south, 0.0)
            fs[:, at(c)] = new_south
            own = tally[:, at(c)]
            tally4 = own + tally[:, at(c, -1)] + tally[:, at(c, -2)] + tally[:, at(c, -3)]
            box = gain * (here + east + surf[:, at(c, 2)] + surf[:, at(c, 3)])
            tally[:, at(c)] = keep * own + number[:, at(c)] * box
            gained[:, at(c)] = keep * gained[:, at(c)] + box
            partial[:, at(c)] = (
                here
                + into * (tally4 - number4[:, at(c)] * here)
                + (TSTEP / CELL) * (north(new_south) - new_south - new_east)
            )
        for c in range(chunks):
            surf[:, at(c)] = partial[:, at(c)] + (TSTEP / CELL) * fe[:, at(c, -1)]
        return carry

    lax.fori_loop(0, STEPS, substep, 0)

    for c in range(chunks):
        lanes = slice(LANES * c, LANES * (c + 1))
        depth_out[:, lanes] = surf[:rows, at(c)] - bed[:rows, at(c)]
        east_out[:, lanes] = fe[:rows, at(c)]
        south_out[:, lanes] = fs[:rows, at(c)]

    flat = jnp.concatenate(
        [jnp.where(row_id < rows, gained[:, at(c)], 0.0) for c in range(chunks)]
        + ([jnp.zeros((blocks_pad - blocks, LANES), jnp.float32)] if blocks_pad > blocks else []),
        axis=0,
    )
    near = slice(owned, 4 * owned)
    turned = jnp.concatenate(thirds(flat.T), axis=0).astype(jnp.bfloat16)
    picked = jnp.dot(turned, hit[:, near], preferred_element_type=jnp.float32)
    picked = picked[:LANES] + picked[LANES : 2 * LANES] + picked[2 * LANES :]
    picked = jnp.sum(jnp.where(lane_hit[:, near], picked, 0.0), axis=0, keepdims=True)
    inside = (valid & (row < rows))[:, near]
    final = jnp.where(inside, keep**STEPS * section[:, near] + picked, 0.0)
    for i in range(3):
        part_out[i] = final[:, i * owned : (i + 1) * owned]


def run_steps(table, pos, depth, flux_east, flux_south, bed, rough, below, above, nodes):
    rows, columns = depth.shape
    owned = nodes.shape[2]
    ext = rows + 2 * HALO
    vmem = pl.BlockSpec(memory_space=pltpu.VMEM)
    smem = pl.BlockSpec(memory_space=pltpu.SMEM)
    tile = jax.ShapeDtypeStruct((rows, columns), jnp.float32)
    return pl.pallas_call(
        steps_kernel,
        out_shape=[tile, tile, tile, jax.ShapeDtypeStruct((3, 1, owned), jnp.float32)],
        in_specs=[smem, smem] + [vmem] * 8,
        out_specs=[vmem] * 4,
        scratch_shapes=[pltpu.VMEM((ext, columns + 2 * LANES), jnp.float32)] * 14,
        compiler_params=pltpu.CompilerParams(vmem_limit_bytes=VMEM_BYTES),
        name="substeps",
    )(table, pos, depth, flux_east, flux_south, bed, rough, below, above, nodes)


def return_kernel(part, out, low, high, ssem, rsem):
    me = lax.axis_index("gy")
    count = lax.axis_size("gy")
    has_prev = me > 0
    has_next = me < count - 1
    barrier = pltpu.get_barrier_semaphore()

    @pl.when(has_prev)
    def _():
        pl.semaphore_signal(barrier, inc=1, device_id={"gy": me - 1}, device_id_type=MESH)

    @pl.when(has_next)
    def _():
        pl.semaphore_signal(barrier, inc=1, device_id={"gy": me + 1}, device_id_type=MESH)

    pl.semaphore_wait(barrier, jnp.minimum(me, 1) + jnp.minimum(count - 1 - me, 1))

    to_prev = send(part.at[0], high, ssem.at[0], rsem.at[0], me - 1)
    to_next = send(part.at[2], low, ssem.at[1], rsem.at[1], me + 1)

    @pl.when(has_prev)
    def _():
        to_prev.start()

    @pl.when(has_next)
    def _():
        to_next.start()

    out[...] = part[1]

    @pl.when(has_next)
    def _():
        to_prev.wait_recv()
        out[...] += high[...]

    @pl.when(has_prev)
    def _():
        to_next.wait_recv()
        out[...] += low[...]

    @pl.when(has_prev)
    def _():
        to_prev.wait_send()

    @pl.when(has_next)
    def _():
        to_next.wait_send()


def return_parts(part):
    shape = part.shape[1:]
    vmem = pl.BlockSpec(memory_space=pltpu.VMEM)
    return pl.pallas_call(
        return_kernel,
        out_shape=jax.ShapeDtypeStruct(shape, jnp.float32),
        in_specs=[vmem],
        out_specs=vmem,
        scratch_shapes=[pltpu.VMEM(shape, jnp.float32)] * 2
        + [pltpu.SemaphoreType.DMA((2,)), pltpu.SemaphoreType.DMA((2,))],
        compiler_params=pltpu.CompilerParams(collective_id=1, has_side_effects=True),
        name="return_parts",
    )(part)


def local(
    depth, flux_east, flux_south, river_section, bed_level, rough_class, manning_table, bank_cell
):
    owned = river_section.shape[0]
    tiles = lax.axis_size("gy")
    pos = jnp.stack([lax.axis_index("gy").astype(jnp.int32), jnp.int32(tiles)])
    below, above, nodes = exchange(
        (depth, flux_east, flux_south, bed_level, rough_class),
        river_section.reshape(1, owned),
        bank_cell,
    )
    depth, flux_east, flux_south, part = run_steps(
        manning_table,
        pos,
        depth,
        flux_east,
        flux_south,
        bed_level,
        rough_class,
        below,
        above,
        nodes,
    )
    return depth, flux_east, flux_south, return_parts(part).reshape(owned)


def solution(mesh):
    return jax.shard_map(
        local,
        mesh=mesh,
        in_specs=(
            P(("runs", "gy"), None),
            P(("runs", "gy"), None),
            P(("runs", "gy"), None),
            P(("runs", "gy")),
            P("gy", None),
            P("gy", None),
            P(),
            P(None, "gy"),
        ),
        out_specs=(
            P(("runs", "gy"), None),
            P(("runs", "gy"), None),
            P(("runs", "gy"), None),
            P(("runs", "gy")),
        ),
        check_vma=False,
    )
```

profile of v0, /device:TPU:1, one launch (start us, length us, event | category | flops | bytes accessed | tf_op | source)
XLA Modules:
  0.0 31.0 jit_solution(3484478713557313216)
XLA Ops:
  0.6 0.1 pad_add_fusion.pos
  0.7 0.0 copy-start
  0.7 0.0 copy-start.1
  0.7 0.0 copy-start.2
  0.7 0.0 copy-start.3
  0.7 0.0 copy-start.4
  0.7 9.1 %exchange.1 = (f32[5,4,1920]{2,1,0:T(4,128)}, f32[5,4,1920]{2,1,0:T(4,128)}, f32[5,2,128]{2,1,0:T(2,128)}) custom-call(f32[32,1920]{1,0:T(8,128)} %depth.1, f32[32,1920]{1,0:T(8,128)} %flux_east.1, f32[32,1920]{1,0:T(8,128)} %flux_south.1, f32[32,1920]{1,0:T(8,128)} %bed_in.1, s32[32,1920]{1,0:T(8,128)} %rough_in.1, f32[32,1920]{1,0:T(8,128)} %depth.1, ...), custom_call_target="tpu_custom_call" | custom-call | tf_op jit(solution)/shard_map/exchange/pallas_call | solution.py:137
  9.9 0.0 copy-start.7
  9.9 0.0 copy-start.9
  9.9 0.0 copy-done
  9.9 0.0 copy-done.1
  9.9 0.0 copy-done.2
  9.9 0.0 copy-done.3
  9.9 0.0 copy-done.4
  9.9 0.6 %copy-done.7 = f32[5,2,128]{2,1,0:T(2,128)S(1)} copy-done((f32[5,2,128]{2,1,0:T(2,128)S(1)}, f32[5,2,128]{2,1,0:T(2,128)}, u32[]{:S(2)}) %copy-start.7) | copy-done | bytes 5144
  10.6 0.0 copy-done.9
  10.6 0.9 %copy-done.5 = f32[5,4,1920]{2,1,0:T(4,128)S(1)} copy-done((f32[5,4,1920]{2,1,0:T(4,128)S(1)}, f32[5,4,1920]{2,1,0:T(4,128)}, u32[]{:S(2)}) %copy-start.5) | copy-done | bytes 153624
  11.5 0.9 %copy-done.6 = f32[5,4,1920]{2,1,0:T(4,128)S(1)} copy-done((f32[5,4,1920]{2,1,0:T(4,128)S(1)}, f32[5,4,1920]{2,1,0:T(4,128)}, u32[]{:S(2)}) %copy-start.6) | copy-done | bytes 153624
  12.4 12.5 %substeps.1 = (f32[32,1920]{1,0:T(8,128)}, f32[32,1920]{1,0:T(8,128)}, f32[32,1920]{1,0:T(8,128)}, f32[3,1,128]{2,1,0:T(1,128)S(1)}) custom-call(f32[8]{0:T(128)S(1)} %copy-done.9, s32[2]{0:T(128)S(1)} %pad_add_fusion.pos, f32[32,1920]{1,0:T(8,128)S(1)} %copy-done, f32[32,1920]{1,0:T(8,128)S(1)} %copy-done.1, f32[32,1920]{1,0:T(8,128)S(1)} %copy-done.2, ...), custom_call_target="tpu_custom_call" | custom-call | tf_op jit(solution)/shard_map/substeps/pallas_call | solution.py:355
  24.9 0.6 %copy-done.8 = f32[3,1,128]{2,1,0:T(1,128)} copy-done((f32[3,1,128]{2,1,0:T(1,128)}, f32[3,1,128]{2,1,0:T(1,128)S(1)}, u32[]{:S(2)}) %copy-start.8) | copy-done | bytes 1560
  25.5 4.4 %return_parts.1 = f32[1,128]{1,0:T(1,128)} custom-call(f32[3,1,128]{2,1,0:T(1,128)} %copy-done.8), custom_call_target="tpu_custom_call" | custom-call | tf_op jit(solution)/shard_map/return_parts/pallas_call | solution.py:418
  29.8 0.0 copy-start.10
  29.8 0.6 %copy-done.10 = f32[1,128]{1,0:T(1,128)S(1)} copy-done((f32[1,128]{1,0:T(1,128)S(1)}, f32[1,128]{1,0:T(1,128)}, u32[]{:S(2)}) %copy-start.10) | copy-done | bytes 536
  30.4 0.5 %copy.13 = f32[128]{0:T(128)} copy(f32[128]{0:T(128)S(1)} %bitcast.4) | data formatting | bytes 1024
  (3 shorter events, 0.0 us)
Async XLA Ops:
  0.7 9.2 %copy-start = (f32[32,1920]{1,0:T(8,128)S(1)}, f32[32,1920]{1,0:T(8,128)}, u32[]{:S(2)}) copy-start(f32[32,1920]{1,0:T(8,128)} %depth.1) | copy-start | bytes 737284
  0.7 9.2 %copy-start.1 = (f32[32,1920]{1,0:T(8,128)S(1)}, f32[32,1920]{1,0:T(8,128)}, u32[]{:S(2)}) copy-start(f32[32,1920]{1,0:T(8,128)} %flux_east.1) | copy-start | bytes 737284
  0.7 9.2 %copy-start.2 = (f32[32,1920]{1,0:T(8,128)S(1)}, f32[32,1920]{1,0:T(8,128)}, u32[]{:S(2)}) copy-start(f32[32,1920]{1,0:T(8,128)} %flux_south.1) | copy-start | bytes 737284
  0.7 9.2 %copy-start.3 = (f32[32,1920]{1,0:T(8,128)S(1)}, f32[32,1920]{1,0:T(8,128)}, u32[]{:S(2)}) copy-start(f32[32,1920]{1,0:T(8,128)} %bed_in.1) | copy-start | bytes 737284
  0.7 9.2 %copy-start.4 = (s32[32,1920]{1,0:T(8,128)S(1)}, s32[32,1920]{1,0:T(8,128)}, u32[]{:S(2)}) copy-start(s32[32,1920]{1,0:T(8,128)} %rough_in.1) | copy-start | bytes 737284
  9.9 0.7 %copy-start.7 = (f32[5,2,128]{2,1,0:T(2,128)S(1)}, f32[5,2,128]{2,1,0:T(2,128)}, u32[]{:S(2)}) copy-start(f32[5,2,128]{2,1,0:T(2,128)} %get-tuple-element.13.nodes) | copy-start | bytes 15364
  9.9 0.7 %copy-start.9 = (f32[8]{0:T(128)S(1)}, f32[8]{0:T(128)}, u32[]{:S(2)}) copy-start(f32[8]{0:T(128)} %table.1) | copy-start | bytes 100
  10.6 0.9 %copy-start.5 = (f32[5,4,1920]{2,1,0:T(4,128)S(1)}, f32[5,4,1920]{2,1,0:T(4,128)}, u32[]{:S(2)}) copy-start(f32[5,4,1920]{2,1,0:T(4,128)} %get-tuple-element.11.below) | copy-start | bytes 460804
  11.5 0.9 %copy-start.6 = (f32[5,4,1920]{2,1,0:T(4,128)S(1)}, f32[5,4,1920]{2,1,0:T(4,128)}, u32[]{:S(2)}) copy-start(f32[5,4,1920]{2,1,0:T(4,128)} %get-tuple-element.12.above) | copy-start | bytes 460804
  24.9 0.6 %copy-start.8 = (f32[3,1,128]{2,1,0:T(1,128)}, f32[3,1,128]{2,1,0:T(1,128)S(1)}, u32[]{:S(2)}) copy-start(f32[3,1,128]{2,1,0:T(1,128)S(1)} %get-tuple-element.17.part) | copy-start | bytes 4612
  29.8 0.6 %copy-start.10 = (f32[1,128]{1,0:T(1,128)S(1)}, f32[1,128]{1,0:T(1,128)}, u32[]{:S(2)}) copy-start(f32[1,128]{1,0:T(1,128)} %return_parts.1) | copy-start | bytes 1540
where the time goes:
time: 31.2 us; the launch traced here: 31 us
  Pallas kernels  26 us (83%)
  local copies, waits for them, and re-layouts  4.14 us (13%)
  between operations  0.73 us (2%)
    pallas_call x1, Pallas kernels, run_steps(): pl.pallas_call(steps_kernel, out_shape=[tile, tile, tile, jax.ShapeDtypeS...  12.5 us
    pallas_call x1, Pallas kernels, exchange(): pl.pallas_call(exchange_kernel, grid=(1,), out_shape=[jax.ShapeDtypeStruc...  9.13 us
    pallas_call x1, Pallas kernels, return_parts(): pl.pallas_call(return_kernel, out_shape=jax.ShapeDtypeStruct(shape, jnp.f...  4.37 us
    unnamed x23, local copies, waits for them, and re-layouts  4.14 us

commit v1 on v0

v1 whole, which is shorter than its diff:
```python
import jax
import jax.numpy as jnp
from jax import lax
from jax.experimental import pallas as pl
from jax.experimental.pallas import tpu as pltpu
from jax.sharding import PartitionSpec as P

STEPS = 4
HALO = STEPS
LANES = 128

GRAV = 9.81
TSTEP = 8.0
CELL = 90.0
FLOOR = 0.05
BANK_COEF = 200.0
CELL_AREA = 8100.0
NODE_AREA = 20000.0

MESH = pl.DeviceIdType.MESH
VMEM_BYTES = 63 * 1024 * 1024
FAR = -float(1 << 24)


def send(src, dst, send_sem, recv_sem, target):
    return pltpu.make_async_remote_copy(
        src_ref=src,
        dst_ref=dst,
        send_sem=send_sem,
        recv_sem=recv_sem,
        device_id={"gy": target},
        device_id_type=MESH,
    )


def thirds(value):
    high = value.astype(jnp.bfloat16).astype(jnp.float32)
    rest = value - high
    mid = rest.astype(jnp.bfloat16).astype(jnp.float32)
    return high, mid, rest - mid


def flood_kernel(
    table,
    depth,
    flux_east,
    flux_south,
    bed_in,
    rough_in,
    section_in,
    cells_in,
    depth_out,
    east_out,
    south_out,
    section_out,
    surf,
    fe,
    fs,
    bed,
    mann,
    max_e,
    max_s,
    drag_e,
    drag_s,
    tally,
    number,
    number4,
    gained,
    partial,
    rough_own,
    up,
    down,
    below,
    above,
    mine,
    nodes,
    part,
    low,
    high,
    in_sem,
    out_sem,
    strip_ssem,
    strip_rsem,
    node_ssem,
    node_rsem,
    part_ssem,
    part_rsem,
):
    me = lax.axis_index("gy")
    tiles = lax.axis_size("gy")
    rows, columns = depth.shape
    ext = rows + 2 * HALO
    chunks = columns // LANES
    owned = nodes.shape[2]
    keep = 1.0 - TSTEP * BANK_COEF * 4.0 / NODE_AREA
    gain = TSTEP * BANK_COEF / NODE_AREA
    into = TSTEP * BANK_COEF / CELL_AREA
    offsets = (-2, -1, 1, 2)

    def there(offset):
        return (me + offset >= 0) & (me + offset < tiles)

    def absent(offset):
        return jnp.logical_not(there(offset))

    barrier = pltpu.get_barrier_semaphore()
    for offset in offsets:
        @pl.when(there(offset))
        def _():
            pl.semaphore_signal(
                barrier, inc=1, device_id={"gy": me + offset}, device_id_type=MESH
            )

    inner = slice(LANES, LANES + columns)
    loads = [
        pltpu.make_async_copy(source, target, in_sem.at[i])
        for i, (source, target) in enumerate(
            (
                (depth, surf.at[:rows, inner]),
                (flux_east, fe.at[:rows, inner]),
                (flux_south, fs.at[:rows, inner]),
                (bed_in, bed.at[:rows, inner]),
                (rough_in, rough_own),
            )
        )
    ]
    for load in loads:
        load.start()
    mine[0:1, :] = section_in[...]
    mine[1:2, :] = cells_in[0:1, :].astype(jnp.float32)

    def at(chunk, shift=0):
        start = LANES * (chunk + 1) + shift
        return slice(start, start + LANES)

    def south(value):
        return pltpu.roll(value, ext - 1, 0)

    def north(value):
        return pltpu.roll(value, 1, 0)

    for ref in (surf, fe, bed, mann, tally, number):
        ref[:, :LANES] = jnp.zeros((ext, LANES), jnp.float32)
        ref[:, LANES * (chunks + 1) :] = jnp.zeros((ext, LANES), jnp.float32)

    for load in loads:
        load.wait()
    for i, ref in enumerate((surf, fe, fs, bed)):
        up[i] = ref[:HALO, inner]
        down[i] = ref[rows - HALO : rows, inner]
    up[4] = rough_own[:HALO, :].astype(jnp.float32)
    down[4] = rough_own[rows - HALO :, :].astype(jnp.float32)

    to_prev = send(up, below, strip_ssem.at[0], strip_rsem.at[0], me - 1)
    to_next = send(down, above, strip_ssem.at[1], strip_rsem.at[1], me + 1)
    to_nodes = [
        send(mine, nodes.at[offset + 2], node_ssem.at[i], node_rsem.at[i], me - offset)
        for i, offset in enumerate(offsets)
    ]
    pl.semaphore_wait(barrier, jnp.minimum(me, 2) + jnp.minimum(tiles - 1 - me, 2))
    for i, offset in enumerate(offsets):
        @pl.when(there(-offset))
        def _():
            to_nodes[i].start()

    @pl.when(there(-1))
    def _():
        to_prev.start()

    @pl.when(there(1))
    def _():
        to_next.start()

    def roughness(rough):
        value = jnp.zeros(rough.shape, jnp.float32)
        for klass in range(table.shape[0]):
            value = jnp.where(rough == float(klass), table[klass], value)
        return value

    for c in range(chunks):
        lanes = slice(LANES * c, LANES * (c + 1))
        mann[:rows, at(c)] = roughness(rough_own[:, lanes].astype(jnp.float32))
        surf[:rows, at(c)] = surf[:rows, at(c)] + bed[:rows, at(c)]
        gained[:, at(c)] = jnp.zeros((ext, LANES), jnp.float32)

    def faces_east(span):
        for c in range(chunks):
            max_e[span, at(c)] = jnp.maximum(bed[span, at(c)], bed[span, at(c, 1)])
            mean_e = 0.5 * (mann[span, at(c)] + mann[span, at(c, 1)])
            drag_e[span, at(c)] = GRAV * TSTEP * mean_e * mean_e

    faces_east(slice(0, rows))

    nodes[2] = mine[...]
    for i, offset in enumerate(offsets):
        @pl.when(there(offset))
        def _():
            to_nodes[i].wait_recv()

        @pl.when(absent(offset))
        def _():
            nodes[offset + 2, 0:1, :] = jnp.zeros((1, owned), jnp.float32)
            nodes[offset + 2, 1:2, :] = jnp.full((1, owned), FAR, jnp.float32)

    row_id = lax.broadcasted_iota(jnp.int32, (ext, LANES), 0)
    lane_id = lax.broadcasted_iota(jnp.int32, (ext, LANES), 1)
    south_open = jnp.logical_not(
        ((row_id == ext - 1) & (me == 0)) | ((row_id == rows - 1) & (me == tiles - 1))
    )

    section = jnp.concatenate([nodes[i, 0:1, :] for i in range(5)], axis=1)
    cell = jnp.concatenate([nodes[i, 1:2, :] for i in range(5)], axis=1).astype(jnp.int32)
    local = cell - (me * rows - HALO) * columns
    valid = (local >= 0) & (local < ext * columns)
    local = jnp.where(valid, local, 0)
    from_top = ((local.astype(jnp.float32) + 0.5) * (1.0 / columns)).astype(jnp.int32)
    column = local - from_top * columns
    row = jnp.where(from_top < HALO, from_top + ext - HALO, from_top - HALO)
    place = jnp.where(valid, (column >> 7) * ext + row, -1)
    lane = column & (LANES - 1)
    total = 5 * owned
    blocks = chunks * ext
    blocks_pad = -(-blocks // LANES) * LANES
    hit = (lax.broadcasted_iota(jnp.int32, (blocks_pad, total), 0) == place)
    hit = jnp.where(hit, 1.0, 0.0).astype(jnp.bfloat16)
    lane_hit = lax.broadcasted_iota(jnp.int32, (LANES, total), 0) == lane
    parts = [jnp.where(lane_hit, part, 0.0) for part in thirds(section)]
    parts.append(jnp.where(lane_hit, 1.0, 0.0))
    weights = jnp.concatenate(parts, axis=0).astype(jnp.bfloat16)
    spread = lax.dot_general(
        hit, weights, (((1,), (1,)), ((), ())), preferred_element_type=jnp.float32
    )
    for c in range(chunks):
        block = spread[c * ext : (c + 1) * ext]
        tally[:, at(c)] = (
            block[:, :LANES] + block[:, LANES : 2 * LANES] + block[:, 2 * LANES : 3 * LANES]
        )
        number[:, at(c)] = block[:, 3 * LANES :]
    for c in range(chunks):
        number4[:, at(c)] = (
            number[:, at(c)] + number[:, at(c, -1)] + number[:, at(c, -2)] + number[:, at(c, -3)]
        )

    @pl.when(there(1))
    def _():
        to_prev.wait_recv()

    @pl.when(absent(1))
    def _():
        below[...] = jnp.zeros_like(below)

    @pl.when(there(-1))
    def _():
        to_next.wait_recv()

    @pl.when(absent(-1))
    def _():
        above[...] = jnp.zeros_like(above)

    outer = slice(rows, ext)
    for c in range(chunks):
        lanes = slice(LANES * c, LANES * (c + 1))
        halo = [
            jnp.concatenate([below[i, :, lanes], above[i, :, lanes]], axis=0) for i in range(5)
        ]
        surf[outer, at(c)] = halo[0] + halo[3]
        fe[outer, at(c)] = halo[1]
        fs[outer, at(c)] = halo[2]
        bed[outer, at(c)] = halo[3]
        mann[outer, at(c)] = roughness(halo[4])
    faces_east(outer)
    for c in range(chunks):
        bed_c, mann_c = bed[:, at(c)], mann[:, at(c)]
        max_s[:, at(c)] = jnp.maximum(bed_c, south(bed_c))
        mean_s = 0.5 * (mann_c + south(mann_c))
        drag_s[:, at(c)] = GRAV * TSTEP * mean_s * mean_s

    def face(flux, surf_a, surf_b, bed_top, drag):
        flow_depth = jnp.maximum(jnp.maximum(surf_a, surf_b) - bed_top, FLOOR)
        driven = flux - (GRAV * TSTEP / CELL) * flow_depth * (surf_b - surf_a)
        damping = 1.0 + drag * jnp.abs(flux) * jnp.exp(jnp.log(flow_depth) * (-7.0 / 3.0))
        return driven / damping

    def substep(_, carry):
        for c in reversed(range(chunks)):
            here = surf[:, at(c)]
            east = surf[:, at(c, 1)]
            new_east = face(fe[:, at(c)], here, east, max_e[:, at(c)], drag_e[:, at(c)])
            if c == chunks - 1:
                new_east = jnp.where(lane_id == LANES - 1, 0.0, new_east)
            fe[:, at(c)] = new_east
            new_south = face(
                fs[:, at(c)], here, south(here), max_s[:, at(c)], drag_s[:, at(c)]
            )
            new_south = jnp.where(south_open, new_south, 0.0)
            fs[:, at(c)] = new_south
            own = tally[:, at(c)]
            tally4 = own + tally[:, at(c, -1)] + tally[:, at(c, -2)] + tally[:, at(c, -3)]
            box = gain * (here + east + surf[:, at(c, 2)] + surf[:, at(c, 3)])
            tally[:, at(c)] = keep * own + number[:, at(c)] * box
            gained[:, at(c)] = keep * gained[:, at(c)] + box
            partial[:, at(c)] = (
                here
                + into * (tally4 - number4[:, at(c)] * here)
                + (TSTEP / CELL) * (north(new_south) - new_south - new_east)
            )
        for c in range(chunks):
            surf[:, at(c)] = partial[:, at(c)] + (TSTEP / CELL) * fe[:, at(c, -1)]
        return carry

    lax.fori_loop(0, STEPS, substep, 0)

    store_east = pltpu.make_async_copy(fe.at[:rows, inner], east_out, out_sem.at[0])
    store_south = pltpu.make_async_copy(fs.at[:rows, inner], south_out, out_sem.at[1])
    store_depth = pltpu.make_async_copy(
        partial.at[:rows, inner], depth_out, out_sem.at[2]
    )
    store_east.start()
    store_south.start()

    flat = jnp.concatenate(
        [jnp.where(row_id < rows, gained[:, at(c)], 0.0) for c in range(chunks)]
        + ([jnp.zeros((blocks_pad - blocks, LANES), jnp.float32)] if blocks_pad > blocks else []),
        axis=0,
    )
    near = slice(owned, 4 * owned)
    turned = jnp.concatenate(thirds(flat.T), axis=0).astype(jnp.bfloat16)
    picked = jnp.dot(turned, hit[:, near], preferred_element_type=jnp.float32)
    picked = picked[:LANES] + picked[LANES : 2 * LANES] + picked[2 * LANES :]
    picked = jnp.sum(jnp.where(lane_hit[:, near], picked, 0.0), axis=0, keepdims=True)
    inside = (valid & (row < rows))[:, near]
    final = jnp.where(inside, keep**STEPS * section[:, near] + picked, 0.0)
    for i in range(3):
        part[i] = final[:, i * owned : (i + 1) * owned]

    part_prev = send(part.at[0], high, part_ssem.at[0], part_rsem.at[0], me - 1)
    part_next = send(part.at[2], low, part_ssem.at[1], part_rsem.at[1], me + 1)

    @pl.when(there(-1))
    def _():
        part_prev.start()

    @pl.when(there(1))
    def _():
        part_next.start()

    for c in range(chunks):
        partial[:rows, at(c)] = surf[:rows, at(c)] - bed[:rows, at(c)]
    store_depth.start()
    section_out[...] = part[1]

    @pl.when(there(-1))
    def _():
        to_prev.wait_send()

    @pl.when(there(1))
    def _():
        to_next.wait_send()

    for i, offset in enumerate(offsets):
        @pl.when(there(-offset))
        def _():
            to_nodes[i].wait_send()

    @pl.when(there(1))
    def _():
        part_prev.wait_recv()
        section_out[...] += high[...]

    @pl.when(there(-1))
    def _():
        part_next.wait_recv()
        section_out[...] += low[...]

    @pl.when(there(-1))
    def _():
        part_prev.wait_send()

    @pl.when(there(1))
    def _():
        part_next.wait_send()

    store_east.wait()
    store_south.wait()
    store_depth.wait()


def local(
    depth, flux_east, flux_south, river_section, bed_level, rough_class, manning_table, bank_cell
):
    rows, columns = depth.shape
    owned = river_section.shape[0]
    ext = rows + 2 * HALO
    anywhere = pl.BlockSpec(memory_space=pltpu.MemorySpace.HBM)
    vmem = pl.BlockSpec(memory_space=pltpu.VMEM)
    smem = pl.BlockSpec(memory_space=pltpu.SMEM)
    tile = jax.ShapeDtypeStruct((rows, columns), jnp.float32)
    strip = pltpu.VMEM((5, HALO, columns), jnp.float32)
    line = pltpu.VMEM((1, owned), jnp.float32)
    dma = pltpu.SemaphoreType.DMA
    depth, flux_east, flux_south, section = pl.pallas_call(
        flood_kernel,
        out_shape=[tile, tile, tile, jax.ShapeDtypeStruct((1, owned), jnp.float32)],
        in_specs=[smem] + [anywhere] * 5 + [vmem] * 2,
        out_specs=[anywhere] * 3 + [vmem],
        scratch_shapes=[pltpu.VMEM((ext, columns + 2 * LANES), jnp.float32)] * 14
        + [pltpu.VMEM((rows, columns), jnp.int32)]
        + [strip] * 4
        + [
            pltpu.VMEM((2, owned), jnp.float32),
            pltpu.VMEM((5, 2, owned), jnp.float32),
            pltpu.VMEM((3, 1, owned), jnp.float32),
            line,
            line,
            dma((5,)),
            dma((3,)),
            dma((2,)),
            dma((2,)),
            dma((4,)),
            dma((4,)),
            dma((2,)),
            dma((2,)),
        ],
        compiler_params=pltpu.CompilerParams(
            collective_id=0, has_side_effects=True, vmem_limit_bytes=VMEM_BYTES
        ),
        name="flood",
    )(
        manning_table,
        depth,
        flux_east,
        flux_south,
        bed_level,
        rough_class,
        river_section.reshape(1, owned),
        bank_cell,
    )
    return depth, flux_east, flux_south, section.reshape(owned)


def solution(mesh):
    return jax.shard_map(
        local,
        mesh=mesh,
        in_specs=(
            P(("runs", "gy"), None),
            P(("runs", "gy"), None),
            P(("runs", "gy"), None),
            P(("runs", "gy")),
            P("gy", None),
            P("gy", None),
            P(),
            P(None, "gy"),
        ),
        out_specs=(
            P(("runs", "gy"), None),
            P(("runs", "gy"), None),
            P(("runs", "gy"), None),
            P(("runs", "gy")),
        ),
        check_vma=False,
    )
```

time: 31.2 us -> 26.5 us (0.85)
  Pallas kernels: 26 us -> 21.7 us
    pallas_call x3 -> x1, Pallas kernels: 26 us -> 21.7 us  [local(): pl.pallas_call(flood_kernel, out_shape=[tile, tile, tile, jax.ShapeDtypeS...]
    unnamed x23 -> x10, local copies, waits for them, and re-layouts: 4.14 us -> 3.94 us
where the time goes in v1:
time: 26.5 us; the launch traced here: 26.3 us
  Pallas kernels  21.7 us (82%)
  local copies, waits for them, and re-layouts  3.94 us (15%)
  between operations  0.65 us (2%)
    pallas_call x1, Pallas kernels, local(): pl.pallas_call(flood_kernel, out_shape=[tile, tile, tile, jax.ShapeDtypeS...  21.7 us
    unnamed x10, local copies, waits for them, and re-layouts  3.94 us

profile of v1, /device:TPU:1, one launch (start us, length us, event | category | flops | bytes accessed | tf_op | source)
XLA Modules:
  0.0 26.3 jit_solution(15314333530959097327)
XLA Ops:
  0.6 21.7 %flood.1 = (f32[32,1920]{1,0:T(8,128)}, f32[32,1920]{1,0:T(8,128)}, f32[32,1920]{1,0:T(8,128)}, f32[1,128]{1,0:T(1,128)}) custom-call(f32[8]{0:T(128)} %table.1, f32[32,1920]{1,0:T(8,128)} %depth.1, f32[32,1920]{1,0:T(8,128)} %flux_east.1, f32[32,1920]{1,0:T(8,128)} %flux_south.1, f32[32,1920]{1,0:T(8,128)} %bed_in.1, s32[32,1920]{1,0:T(8,128)} %rough_in.1, ...), custom_call_target="tpu_custom_call" | custom-call | tf_op jit(solution)/shard_map/flood/pallas_call | solution.py:401
  22.3 0.0 copy-start.1
  22.3 1.7 %copy.16 = f32[32,1920]{1,0:T(8,128)} copy(f32[32,1920]{1,0:T(8,128)} %get-tuple-element.16) | data formatting | bytes 491520
  24.0 0.0 copy-done.1
  24.0 0.0 copy-start
  24.0 0.7 %copy.17 = f32[32,1920]{1,0:T(8,128)} copy(f32[32,1920]{1,0:T(8,128)S(1)} %copy-done.1) | data formatting | bytes 491520
  24.7 0.3 %copy-done = f32[32,1920]{1,0:T(8,128)S(1)} copy-done((f32[32,1920]{1,0:T(8,128)S(1)}, f32[32,1920]{1,0:T(8,128)}, u32[]{:S(2)}) %copy-start) | copy-done | bytes 245784
  25.1 0.0 copy-start.2
  25.1 0.7 %copy.18 = f32[32,1920]{1,0:T(8,128)} copy(f32[32,1920]{1,0:T(8,128)S(1)} %copy-done) | data formatting | bytes 491520
  25.8 0.0 copy-done.2
  25.8 0.5 %copy.19 = f32[128]{0:T(128)} copy(f32[128]{0:T(128)S(1)} %bitcast.3) | data formatting | bytes 1024
Async XLA Ops:
  22.3 1.7 %copy-start.1 = (f32[32,1920]{1,0:T(8,128)S(1)}, f32[32,1920]{1,0:T(8,128)}, u32[]{:S(2)}) copy-start(f32[32,1920]{1,0:T(8,128)} %get-tuple-element.17) | copy-start | bytes 737284
  24.0 1.0 %copy-start = (f32[32,1920]{1,0:T(8,128)S(1)}, f32[32,1920]{1,0:T(8,128)}, u32[]{:S(2)}) copy-start(f32[32,1920]{1,0:T(8,128)} %get-tuple-element.18) | copy-start | bytes 737284
  25.1 0.7 %copy-start.2 = (f32[1,128]{1,0:T(1,128)S(1)}, f32[1,128]{1,0:T(1,128)}, u32[]{:S(2)}) copy-start(f32[1,128]{1,0:T(1,128)} %get-tuple-element.11) | copy-start | bytes 1540

commit v2 on v1

--- a/solution.py
+++ b/solution.py
@@ -67,6 +67,7 @@
     number4,
     gained,
     partial,
+    moved,
     rough_own,
     up,
     down,
@@ -208,6 +209,20 @@
         ((row_id == ext - 1) & (me == 0)) | ((row_id == rows - 1) & (me == tiles - 1))
     )
 
+    def later(value, shift, carried):
+        turned = pltpu.roll(value, LANES - shift, 1)
+        return jnp.where(lane_id < LANES - shift, turned, carried), turned
+
+    def earlier(value, shift, carried):
+        turned = pltpu.roll(value, shift, 1)
+        return jnp.where(lane_id >= shift, turned, carried), turned
+
+    def last_four(value, carried):
+        shifted, one = earlier(value, 1, carried[0])
+        pair = value + shifted
+        shifted, two = earlier(pair, 2, carried[1])
+        return pair + shifted, (one, two)
+
     section = jnp.concatenate([nodes[i, 0:1, :] for i in range(5)], axis=1)
     cell = jnp.concatenate([nodes[i, 1:2, :] for i in range(5)], axis=1).astype(jnp.int32)
     local = cell - (me * rows - HALO) * columns
@@ -236,10 +251,11 @@
             block[:, :LANES] + block[:, LANES : 2 * LANES] + block[:, 2 * LANES : 3 * LANES]
         )
         number[:, at(c)] = block[:, 3 * LANES :]
+    summed = (jnp.zeros((ext, LANES), jnp.float32),) * 2
+    counted = summed
     for c in range(chunks):
-        number4[:, at(c)] = (
-            number[:, at(c)] + number[:, at(c, -1)] + number[:, at(c, -2)] + number[:, at(c, -3)]
-        )
+        tally[:, at(c)], summed = last_four(tally[:, at(c)], summed)
+        number4[:, at(c)], counted = last_four(number[:, at(c)], counted)
 
     @pl.when(there(1))
     def _():
@@ -282,9 +298,11 @@
         return driven / damping
 
     def substep(_, carry):
+        blank = jnp.zeros((ext, LANES), jnp.float32)
+        one, two = blank, blank
         for c in reversed(range(chunks)):
             here = surf[:, at(c)]
-            east = surf[:, at(c, 1)]
+            east, one = later(here, 1, one)
             new_east = face(fe[:, at(c)], here, east, max_e[:, at(c)], drag_e[:, at(c)])
             if c == chunks - 1:
                 new_east = jnp.where(lane_id == LANES - 1, 0.0, new_east)
@@ -294,18 +312,23 @@
             )
             new_south = jnp.where(south_open, new_south, 0.0)
             fs[:, at(c)] = new_south
-            own = tally[:, at(c)]
-            tally4 = own + tally[:, at(c, -1)] + tally[:, at(c, -2)] + tally[:, at(c, -3)]
-            box = gain * (here + east + surf[:, at(c, 2)] + surf[:, at(c, 3)])
-            tally[:, at(c)] = keep * own + number[:, at(c)] * box
+            pair = here + east
+            shifted, two = later(pair, 2, two)
+            box = gain * (pair + shifted)
             gained[:, at(c)] = keep * gained[:, at(c)] + box
+            moved[:, at(c)] = number[:, at(c)] * box
             partial[:, at(c)] = (
                 here
-                + into * (tally4 - number4[:, at(c)] * here)
+                + into * (tally[:, at(c)] - number4[:, at(c)] * here)
                 + (TSTEP / CELL) * (north(new_south) - new_south - new_east)
             )
+        west = blank
+        summed = (blank, blank)
         for c in range(chunks):
-            surf[:, at(c)] = partial[:, at(c)] + (TSTEP / CELL) * fe[:, at(c, -1)]
+            from_west, west = earlier(fe[:, at(c)], 1, west)
+            surf[:, at(c)] = partial[:, at(c)] + (TSTEP / CELL) * from_west
+            spill, summed = last_four(moved[:, at(c)], summed)
+            tally[:, at(c)] = keep * tally[:, at(c)] + spill
         return carry
 
     lax.fori_loop(0, STEPS, substep, 0)
@@ -383,6 +406,44 @@
     store_east.wait()
     store_south.wait()
     store_depth.wait()
+
+
+def finish_kernel(a, b, c, d, a_out, b_out, c_out, d_out, held, line, in_sem, out_sem):
+    sources = (a, b, c, d)
+    targets = (a_out, b_out, c_out, d_out)
+    stops = (held.at[0], held.at[1], held.at[2], line)
+    loads = [
+        pltpu.make_async_copy(sources[i], stops[i], in_sem.at[i]) for i in range(4)
+    ]
+    stores = [
+        pltpu.make_async_copy(stops[i], targets[i], out_sem.at[i]) for i in range(4)
+    ]
+    for load in loads:
+        load.start()
+    for load, store in zip(loads, stores):
+        load.wait()
+        store.start()
+    for store in stores:
+        store.wait()
+
+
+def finish(*arrays):
+    anywhere = pl.BlockSpec(memory_space=pltpu.MemorySpace.HBM)
+    dma = pltpu.SemaphoreType.DMA
+    return pl.pallas_call(
+        finish_kernel,
+        out_shape=[jax.ShapeDtypeStruct(a.shape, a.dtype) for a in arrays],
+        in_specs=[anywhere] * 4,
+        out_specs=[anywhere] * 4,
+        scratch_shapes=[
+            pltpu.VMEM((3,) + arrays[0].shape, jnp.float32),
+            pltpu.VMEM(arrays[3].shape, jnp.float32),
+            dma((4,)),
+            dma((4,)),
+        ],
+        compiler_params=pltpu.CompilerParams(vmem_limit_bytes=VMEM_BYTES),
+        name="finish",
+    )(*arrays)
 
 
 def local(
@@ -403,7 +464,7 @@
         out_shape=[tile, tile, tile, jax.ShapeDtypeStruct((1, owned), jnp.float32)],
         in_specs=[smem] + [anywhere] * 5 + [vmem] * 2,
         out_specs=[anywhere] * 3 + [vmem],
-        scratch_shapes=[pltpu.VMEM((ext, columns + 2 * LANES), jnp.float32)] * 14
+        scratch_shapes=[pltpu.VMEM((ext, columns + 2 * LANES), jnp.float32)] * 15
         + [pltpu.VMEM((rows, columns), jnp.int32)]
         + [strip] * 4
         + [
@@ -435,6 +496,7 @@
         river_section.reshape(1, owned),
         bank_cell,
     )
+    depth, flux_east, flux_south, section = finish(depth, flux_east, flux_south, section)
     return depth, flux_east, flux_south, section.reshape(owned)
 
 

time: 26.5 us -> 22.1 us (0.83)
  local copies, waits for them, and re-layouts: 3.94 us -> 0 us
  Pallas kernels: 21.7 us -> 21.3 us
    unnamed x10 -> x0, local copies, waits for them, and re-layouts: 3.94 us -> none
    pallas_call x1, Pallas kernels: 21.7 us -> 19.4 us  [local(): pl.pallas_call(flood_kernel, out_shape=[tile, tile, tile, jax.ShapeDtypeS...]
    pallas_call x0 -> x1, Pallas kernels: none -> 1.95 us  [finish(): pl.pallas_call(finish_kernel, out_shape=[jax.ShapeDtypeStruct(a.shape, a....]
where the time goes in v2:
time: 22.1 us; the launch traced here: 21.9 us
  Pallas kernels  21.3 us (96%)
  between operations  0.64 us (3%)
    pallas_call x1, Pallas kernels, local(): pl.pallas_call(flood_kernel, out_shape=[tile, tile, tile, jax.ShapeDtypeS...  19.4 us
    pallas_call x1, Pallas kernels, finish(): pl.pallas_call(finish_kernel, out_shape=[jax.ShapeDtypeStruct(a.shape, a....  1.95 us

profile of v2, /device:TPU:1, one launch (start us, length us, event | category | flops | bytes accessed | tf_op | source)
XLA Modules:
  0.0 21.9 jit_solution(14978360675619164365)
XLA Ops:
  0.6 19.4 %flood.1 = (f32[32,1920]{1,0:T(8,128)}, f32[32,1920]{1,0:T(8,128)}, f32[32,1920]{1,0:T(8,128)}, f32[1,128]{1,0:T(1,128)}) custom-call(f32[8]{0:T(128)} %table.1, f32[32,1920]{1,0:T(8,128)} %depth.1, f32[32,1920]{1,0:T(8,128)} %flux_east.1, f32[32,1920]{1,0:T(8,128)} %flux_south.1, f32[32,1920]{1,0:T(8,128)} %bed_in.1, s32[32,1920]{1,0:T(8,128)} %rough_in.1, ...), custom_call_target="tpu_custom_call" | custom-call | tf_op jit(solution)/shard_map/flood/pallas_call | solution.py:462
  20.0 1.9 %finish.1 = (f32[32,1920]{1,0:T(8,128)}, f32[32,1920]{1,0:T(8,128)}, f32[32,1920]{1,0:T(8,128)}, f32[1,128]{1,0:T(1,128)}) custom-call(f32[32,1920]{1,0:T(8,128)} %get-tuple-element.12.a, f32[32,1920]{1,0:T(8,128)} %get-tuple-element.13.b, f32[32,1920]{1,0:T(8,128)} %get-tuple-element.14.c, f32[1,128]{1,0:T(1,128)} %get-tuple-element.15.d), custom_call_target="tpu_custom_call" | custom-call | tf_op jit(solution)/shard_map/finish/pallas_call | solution.py:433

commit v3 on v2

--- a/solution.py
+++ b/solution.py
@@ -297,7 +297,7 @@
         damping = 1.0 + drag * jnp.abs(flux) * jnp.exp(jnp.log(flow_depth) * (-7.0 / 3.0))
         return driven / damping
 
-    def substep(_, carry):
+    def substep(_, carry, nodes_too=True):
         blank = jnp.zeros((ext, LANES), jnp.float32)
         one, two = blank, blank
         for c in reversed(range(chunks)):
@@ -312,11 +312,12 @@
             )
             new_south = jnp.where(south_open, new_south, 0.0)
             fs[:, at(c)] = new_south
-            pair = here + east
-            shifted, two = later(pair, 2, two)
-            box = gain * (pair + shifted)
-            gained[:, at(c)] = keep * gained[:, at(c)] + box
-            moved[:, at(c)] = number[:, at(c)] * box
+            if nodes_too:
+                pair = here + east
+                shifted, two = later(pair, 2, two)
+                box = gain * (pair + shifted)
+                gained[:, at(c)] = keep * gained[:, at(c)] + box
+                moved[:, at(c)] = number[:, at(c)] * box
             partial[:, at(c)] = (
                 here
                 + into * (tally[:, at(c)] - number4[:, at(c)] * here)
@@ -327,19 +328,20 @@
         for c in range(chunks):
             from_west, west = earlier(fe[:, at(c)], 1, west)
             surf[:, at(c)] = partial[:, at(c)] + (TSTEP / CELL) * from_west
-            spill, summed = last_four(moved[:, at(c)], summed)
-            tally[:, at(c)] = keep * tally[:, at(c)] + spill
+            if nodes_too:
+                spill, summed = last_four(moved[:, at(c)], summed)
+                tally[:, at(c)] = keep * tally[:, at(c)] + spill
         return carry
 
-    lax.fori_loop(0, STEPS, substep, 0)
-
-    store_east = pltpu.make_async_copy(fe.at[:rows, inner], east_out, out_sem.at[0])
-    store_south = pltpu.make_async_copy(fs.at[:rows, inner], south_out, out_sem.at[1])
-    store_depth = pltpu.make_async_copy(
-        partial.at[:rows, inner], depth_out, out_sem.at[2]
-    )
-    store_east.start()
-    store_south.start()
+    lax.fori_loop(0, STEPS - 1, substep, 0)
+
+    one = two = jnp.zeros((ext, LANES), jnp.float32)
+    for c in reversed(range(chunks)):
+        here = surf[:, at(c)]
+        east, one = later(here, 1, one)
+        pair = here + east
+        shifted, two = later(pair, 2, two)
+        gained[:, at(c)] = keep * gained[:, at(c)] + gain * (pair + shifted)
 
     flat = jnp.concatenate(
         [jnp.where(row_id < rows, gained[:, at(c)], 0.0) for c in range(chunks)]
@@ -366,6 +368,15 @@
     @pl.when(there(1))
     def _():
         part_next.start()
+
+    substep(0, 0, nodes_too=False)
+    store_east = pltpu.make_async_copy(fe.at[:rows, inner], east_out, out_sem.at[0])
+    store_south = pltpu.make_async_copy(fs.at[:rows, inner], south_out, out_sem.at[1])
+    store_depth = pltpu.make_async_copy(
+        partial.at[:rows, inner], depth_out, out_sem.at[2]
+    )
+    store_east.start()
+    store_south.start()
 
     for c in range(chunks):
         partial[:rows, at(c)] = surf[:rows, at(c)] - bed[:rows, at(c)]

time: 22.1 us -> 20.7 us (0.937)
  Pallas kernels: 21.3 us -> 19.9 us
    pallas_call x1, Pallas kernels: 19.4 us -> 17.9 us  [local(): pl.pallas_call(flood_kernel, out_shape=[tile, tile, tile, jax.ShapeDtypeS...]
where the time goes in v3:
time: 20.7 us; the launch traced here: 20.5 us
  Pallas kernels  19.9 us (96%)
  between operations  0.64 us (3%)
    pallas_call x1, Pallas kernels, local(): pl.pallas_call(flood_kernel, out_shape=[tile, tile, tile, jax.ShapeDtypeS...  17.9 us
    pallas_call x1, Pallas kernels, finish(): pl.pallas_call(finish_kernel, out_shape=[jax.ShapeDtypeStruct(a.shape, a....  1.95 us

profile of v3, /device:TPU:1, one launch (start us, length us, event | category | flops | bytes accessed | tf_op | source)
XLA Modules:
  0.0 20.5 jit_solution(5991907439041427131)
XLA Ops:
  0.6 17.9 %flood.1 = (f32[32,1920]{1,0:T(8,128)}, f32[32,1920]{1,0:T(8,128)}, f32[32,1920]{1,0:T(8,128)}, f32[1,128]{1,0:T(1,128)}) custom-call(f32[8]{0:T(128)} %table.1, f32[32,1920]{1,0:T(8,128)} %depth.1, f32[32,1920]{1,0:T(8,128)} %flux_east.1, f32[32,1920]{1,0:T(8,128)} %flux_south.1, f32[32,1920]{1,0:T(8,128)} %bed_in.1, s32[32,1920]{1,0:T(8,128)} %rough_in.1, ...), custom_call_target="tpu_custom_call" | custom-call | tf_op jit(solution)/shard_map/flood/pallas_call | solution.py:473
  18.6 1.9 %finish.1 = (f32[32,1920]{1,0:T(8,128)}, f32[32,1920]{1,0:T(8,128)}, f32[32,1920]{1,0:T(8,128)}, f32[1,128]{1,0:T(1,128)}) custom-call(f32[32,1920]{1,0:T(8,128)} %get-tuple-element.12.a, f32[32,1920]{1,0:T(8,128)} %get-tuple-element.13.b, f32[32,1920]{1,0:T(8,128)} %get-tuple-element.14.c, f32[1,128]{1,0:T(1,128)} %get-tuple-element.15.d), custom_call_target="tpu_custom_call" | custom-call | tf_op jit(solution)/shard_map/finish/pallas_call | solution.py:444
